TPU v7x, 128 devices: a whole 4x4x4 slice. The times are simulated.
128 devices in a mesh: lat: 16 (over y_hi, x, core), lon: 8 (over y_lo, z).
Axes of the slice: x: 4, y: 4 (y_hi: 2, y_lo: 2; y = y_hi * 2 + y_lo), z: 4, core: 2. Of those that a mesh axis runs over, the one named last changes fastest.
Arguments:
- ensemble: float32 [2, 1, 2048, 16384], P(None, None, 'lat', 'lon'), may hold values from -6 to 6
- cross_mix: float32 [2, 2048, 16384], P(None, 'lat', 'lon'), may hold values from -0.5 to 0.5
- sea_mask: int32 [2048, 16384], P('lat', 'lon'), may hold values 0 or 1
- level_rates: float32 [2, 2], replicated, may hold values from 1 to 256, as said below
- panel_inverse: float32 [2, 2, 128, 128], replicated, may hold values from 0 to 1, as said below
- reduced_lon: float32 [2, 256, 256], replicated, as said below
- reduced_lat: float32 [2, 32, 32], replicated, as said below
Outputs:
- smoothed: float32 [2, 1, 2048, 16384], P(None, None, 'lat', 'lon')
Inputs may be any that keep to these rules, and one draw needn't show every extreme that they name: `level_rates`: the same for every point of a level. `panel_inverse`: the inverse of the 128 x 128 tridiagonal matrix whose diagonal entries are one plus twice a (that is 1 + 2*a) and whose entries beside the diagonal are -a, a taken from level_rates. `reduced_lon`: the inverse of the system that the longitude line solve's panel end values satisfy, for the given panel inverses and rates. `reduced_lat`: the inverse of the system that the latitude line solve's panel end values satisfy, for the given panel inverses and rates.
All inputs are finite; a program needn't handle non-finite values. No bound on the sum of `sea_mask` on one device may be relied on, other than what follows from the above.
Results may differ from a plain program's by a relative error of at most 0.00018.
Values sent between devices are 32-bit elements; how exact they have to be, the bound alone decides.
No kernel may reach another device: no remote copies, remote signals or barrier semaphores. Data moves between devices by JAX's collectives and lax.ppermute only.
A program may use at most 128 MiB of HBM per device.

v0:
```python
import jax
import jax.numpy as jnp
from jax import lax
from jax.sharding import PartitionSpec as P

STEPS = 2
highest = lax.Precision.HIGHEST


def with_halo(shard, sides, width, wrap):
    for axis, dim in sides:
        size, length = (lax.axis_size(axis), shard.shape[dim])
        up = [(i, (i + 1) % size) for i in range(size if wrap else size - 1)]
        down = [(j, i) for i, j in up]
        last = lax.slice_in_dim(shard, length - width, length, axis=dim)
        first = lax.slice_in_dim(shard, 0, width, axis=dim)
        before = lax.ppermute(last, axis, up)
        after = lax.ppermute(first, axis, down)
        shard = jnp.concatenate([before, shard, after], axis=dim)
    return shard


def cross_term(extended):
    return (
        extended[:, :, 2:, 2:]
        - extended[:, :, 2:, :-2]
        - extended[:, :, :-2, 2:]
        + extended[:, :, :-2, :-2]
    )


def explicit_terms(extended):
    centre = extended[:, :, 1:-1, 1:-1]
    along_lon = extended[:, :, 1:-1, 2:] - 2.0 * centre + extended[:, :, 1:-1, :-2]
    along_lat = extended[:, :, 2:, 1:-1] - 2.0 * centre + extended[:, :, :-2, 1:-1]
    return (along_lon, along_lat, cross_term(extended))


def lon_panels(values, inverse):
    panel = inverse.shape[1]
    dims = values.shape
    split = values.reshape(dims[:3] + (dims[3] // panel, panel))
    return jnp.einsum("lsrcq,lpq->lsrcp", split, inverse, precision=highest)


def lon_ends(solved):
    paired = jnp.stack((solved[..., 0], solved[..., -1]), axis=-1)
    return paired.reshape(paired.shape[:3] + (-1,))


def lon_finish(solved, prev_last, next_first, inverse, rate_lon):
    left_col = inverse[:, None, None, None, :, 0]
    right_col = inverse[:, None, None, None, :, -1]
    scale = rate_lon[:, None, None, None, None]
    result = solved + scale * (prev_last[..., None] * left_col + next_first[..., None] * right_col)
    return result.reshape(result.shape[:3] + (-1,))


def lon_solve(values, inverse, reduced, rate_lon):
    solved = lon_panels(values, inverse)
    bounds = jnp.einsum("lsrk,lmk->lsrm", lon_ends(solved), reduced, precision=highest)
    pairs = bounds.reshape(bounds.shape[:3] + (-1, 2))
    prev_last = jnp.roll(pairs[..., 1], 1, axis=-1)
    next_first = jnp.roll(pairs[..., 0], -1, axis=-1)
    return lon_finish(solved, prev_last, next_first, inverse, rate_lon)


def lat_panels(values, inverse):
    panel = inverse.shape[1]
    dims = values.shape
    split = values.reshape((dims[0], dims[1], dims[2] // panel, panel, dims[3]))
    return jnp.einsum("lscqw,lpq->lscpw", split, inverse, precision=highest)


def lat_ends(solved):
    paired = jnp.stack((solved[:, :, :, 0, :], solved[:, :, :, -1, :]), axis=3)
    return paired.reshape((paired.shape[0], paired.shape[1], -1, paired.shape[4]))


def lat_shifted(pairs):
    first_end = pairs[:, :, :, 0, :]
    last_end = pairs[:, :, :, 1, :]
    zero_row = jnp.zeros_like(last_end[:, :, :1])
    prev_last = jnp.concatenate((zero_row, last_end[:, :, :-1]), axis=2)
    next_first = jnp.concatenate((first_end[:, :, 1:], zero_row), axis=2)
    return (prev_last, next_first)


def lat_finish(solved, prev_last, next_first, inverse, rate_lat):
    left_col = inverse[:, None, None, :, 0][..., None]
    right_col = inverse[:, None, None, :, -1][..., None]
    scale = rate_lat[:, None, None, None, None]
    result = solved + scale * (
        prev_last[:, :, :, None, :] * left_col + next_first[:, :, :, None, :] * right_col
    )
    dims = result.shape
    return result.reshape((dims[0], dims[1], dims[2] * dims[3], dims[4]))


def lat_solve(values, inverse, reduced, rate_lat):
    solved = lat_panels(values, inverse)
    bounds = jnp.einsum("lskw,lmk->lsmw", lat_ends(solved), reduced, precision=highest)
    dims = bounds.shape
    pairs = bounds.reshape((dims[0], dims[1], -1, 2, dims[3]))
    prev_last, next_first = lat_shifted(pairs)
    return lat_finish(solved, prev_last, next_first, inverse, rate_lat)


def extend_block(values):
    wide = with_halo(values, (("lon", 3),), 1, True)
    return with_halo(wide, (("lat", 2),), 1, False)


def lon_lines_solve(values, inverse, reduced, rate_lon):
    finished = lon_solve(
        lax.all_to_all(values, "lon", split_axis=2, concat_axis=3, tiled=True),
        inverse,
        reduced,
        rate_lon,
    )
    return lax.all_to_all(finished, "lon", split_axis=3, concat_axis=2, tiled=True)


def lat_lines_solve(values, inverse, reduced, rate_lat):
    finished = lat_solve(
        lax.all_to_all(values, "lat", split_axis=3, concat_axis=2, tiled=True),
        inverse,
        reduced,
        rate_lat,
    )
    return lax.all_to_all(finished, "lat", split_axis=2, concat_axis=3, tiled=True)


def shards(ensemble, cross_mix, sea_mask, level_rates, panel_inverse, reduced_lon, reduced_lat):
    sea_float = sea_mask.astype(jnp.float32)[None, None]
    mixing = cross_mix[:, None]
    rate_lon = level_rates[0]
    rate_lat = level_rates[1]
    scale_lon = rate_lon[:, None, None, None]
    scale_lat = rate_lat[:, None, None, None]
    inverse_lon = panel_inverse[0]
    inverse_lat = panel_inverse[1]

    def solve_lon(values):
        return lon_lines_solve(values, inverse_lon, reduced_lon, rate_lon)

    def solve_lat(values):
        return lat_lines_solve(values, inverse_lat, reduced_lat, rate_lat)

    current = ensemble
    for repeat in range(STEPS):
        along_lon, along_lat, diagonal_diff = explicit_terms(extend_block(current))
        start_value = sea_float * (
            current
            + mixing * diagonal_diff
            + 2.0 * scale_lon * along_lon
            + 2.0 * scale_lat * along_lat
        )
        first_lon = solve_lon(start_value - scale_lon * along_lon)
        first_lat = solve_lat(first_lon - scale_lat * along_lat)
        correction = cross_term(extend_block(first_lat - current))
        corrected = start_value + 0.5 * mixing * correction
        second_lon = solve_lon(corrected - scale_lon * along_lon)
        second_lat = solve_lat(second_lon - scale_lat * along_lat)
        current = sea_float * second_lat
    return current


def solution(mesh):
    in_specs = (
        P(None, None, "lat", "lon"),
        P(None, "lat", "lon"),
        P("lat", "lon"),
        P(),
        P(),
        P(),
        P(),
    )
    out_specs = P(None, None, "lat", "lon")
    return jax.shard_map(shards, mesh=mesh, in_specs=in_specs, out_specs=out_specs, check_vma=False)
```

profile of v0, /device:TPU:1, one launch (start us, length us, event | category | flops | bytes accessed | tf_op | source)
XLA Modules:
  0.0 1259.1 jit_solution(113004368854663224)
XLA Ops:
  1.1 5.7 collective-permute-start.1
  24.4 12.4 multiply_subtract_fusion.1
  45.1 26.1 %all-to-all-done = f32[2,1,128,2048]{3,0,1,2:T(2,128)} async-done(((f32[2,1,128,2048]{3,0,1,2:T(2,128)}), f32[2,1,128,2048]{3,0,1,2:T(2,128)}, u32[]{:S(2)}, u32[]{:S(2)}) %all-to-all-start) | async-done | bytes 2097184 | tf_op jit(solution)/shard_map/all_to_all | solution.py:116
  89.3 14.4 %copy.255 = f32[2,16,128,128]{1,0,3,2:T(2,128)} copy(f32[2,16,128,128]{2,3,1,0:T(8,128)} %multiply_add_fusion.7) | data formatting | bytes 4194304 | tf_op jit(solution)/shard_map/reshape | solution.py:56
  103.6 24.7 %reshape.408 = f32[8,1,65536]{2,1,0:T(1,128)} reshape(f32[16384,1,2,16]{3,2,1,0:T(2,128)} %bitcast.331) | data formatting | bytes 4194304
  128.4 30.0 %all_to_all.264 = f32[8,1,65536]{2,1,0:T(1,128)} all-to-all(f32[8,1,65536]{2,1,0:T(1,128)} %reshape.408), channel_id=1, replica_groups=mesh['lat'=16,'lon'=8] {'lon'}, dimensions={0} | all-to-all | bytes 4194304 | tf_op jit(solution)/shard_map/all_to_all | solution.py:121
  158.9 8.5 reduce.8
  167.3 31.9 %reshape.409 = f32[16384,1,2,16]{3,2,1,0:T(2,128)} reshape(f32[8,65536]{1,0:T(8,128)} %reduce.8) | data formatting | bytes 4194304
  199.2 21.6 %copy.257 = f32[2,1,16,8,2048]{4,2,3,0,1:T(8,128)} copy(f32[2,1,16,8,2048]{2,0,4,3,1:T(2,128)} %bitcast.332) | data formatting | bytes 4194304 | tf_op jit(solution)/shard_map/all_to_all | solution.py:121
  229.0 9.3 all-to-all-start.2
  238.5 28.4 %all-to-all-done.2 = f32[2,1,128,2048]{2,0,1,3:T(2,128)} async-done(((f32[2,1,128,2048]{2,0,1,3:T(2,128)}), f32[2,1,128,2048]{2,0,1,3:T(2,128)}, u32[]{:S(2)}, u32[]{:S(2)}) %all-to-all-start.2) | async-done | bytes 2097184 | tf_op jit(solution)/shard_map/all_to_all | solution.py:126
  275.5 7.6 copy.178
  283.1 33.5 %all_to_all.265 = f32[2,1,2048,128]{3,0,1,2:T(2,128)S(1)} all-to-all(f32[2,1,2048,128]{3,0,1,2:T(2,128)S(1)} %copy.178), channel_id=1, replica_groups=mesh['lat'=16,'lon'=8] {'lat'}, dimensions={2} | all-to-all | bytes 4194304 | tf_op jit(solution)/shard_map/all_to_all | solution.py:131
  344.6 10.0 fusion.37
  356.3 28.1 %all_to_all.266 = f32[2,1,128,2048]{3,0,1,2:T(2,128)S(1)} all-to-all(f32[2,1,128,2048]{3,0,1,2:T(2,128)S(1)} %copy.181), channel_id=1, replica_groups=mesh['lat'=16,'lon'=8] {'lon'}, dimensions={2} | all-to-all | bytes 4194304 | tf_op jit(solution)/shard_map/all_to_all | solution.py:116
  400.8 14.4 %copy.260 = f32[2,16,128,128]{1,0,3,2:T(2,128)} copy(f32[2,16,128,128]{2,3,1,0:T(8,128)} %multiply_add_fusion.5) | data formatting | bytes 4194304 | tf_op jit(solution)/shard_map/reshape | solution.py:56
  415.2 24.7 %reshape.410 = f32[8,1,65536]{2,1,0:T(1,128)} reshape(f32[16384,1,2,16]{3,2,1,0:T(2,128)} %bitcast.333) | data formatting | bytes 4194304
  439.9 28.7 %all_to_all.267 = f32[8,1,65536]{2,1,0:T(1,128)} all-to-all(f32[8,1,65536]{2,1,0:T(1,128)} %reshape.410), channel_id=1, replica_groups=mesh['lat'=16,'lon'=8] {'lon'}, dimensions={0} | all-to-all | bytes 4194304 | tf_op jit(solution)/shard_map/all_to_all | solution.py:121
  468.6 8.5 reduce.9
  477.0 32.1 %reshape.411 = f32[16384,1,2,16]{3,2,1,0:T(2,128)} reshape(f32[8,65536]{1,0:T(8,128)} %reduce.9) | data formatting | bytes 4194304
  509.1 21.6 %copy.262 = f32[2,1,16,8,2048]{4,2,3,0,1:T(8,128)} copy(f32[2,1,16,8,2048]{2,0,4,3,1:T(2,128)} %bitcast.334) | data formatting | bytes 4194304 | tf_op jit(solution)/shard_map/all_to_all | solution.py:121
  538.9 37.6 %all_to_all.268 = f32[2,1,128,2048]{2,0,1,3:T(2,128)} all-to-all(f32[2,1,128,2048]{2,0,1,3:T(2,128)} %copy.195), channel_id=1, replica_groups=mesh['lat'=16,'lon'=8] {'lat'}, dimensions={3} | all-to-all | bytes 4194304 | tf_op jit(solution)/shard_map/all_to_all | solution.py:126
  585.1 7.6 copy.200
  592.7 31.8 %all_to_all.269 = f32[2,1,2048,128]{3,0,1,2:T(2,128)S(1)} all-to-all(f32[2,1,2048,128]{3,0,1,2:T(2,128)S(1)} %copy.200), channel_id=1, replica_groups=mesh['lat'=16,'lon'=8] {'lat'}, dimensions={2} | all-to-all | bytes 4194304 | tf_op jit(solution)/shard_map/all_to_all | solution.py:131
  653.5 14.2 %multiply_subtract_fusion = (f32[2,1,128,2048]{3,2,0,1:T(8,128)S(1)}, f32[2,1,128,2048]{3,2,0,1:T(8,128)}) fusion(f32[2]{0:T(128)S(1)} %get-tuple-element.65, f32[2,1,128,2048]{3,2,0,1:T(8,128)} %copy-done.2, f32[2,1,128,1]{3,2,0,1:T(8,128)S(1)} %collective-permute-done.8, f32[2,1,128,1]{3,2,0,1:T(8,128)S(1)} %collective-permute-done.9, ...), kind=kLoop, calls=%fused_computation.109 | loop fusion | flops 13107200 | bytes 11571256 | tf_op jit(solution)/shard_map/sub | solution.py:159
  669.3 28.4 %all_to_all.270 = f32[2,1,128,2048]{3,0,1,2:T(2,128)S(1)} all-to-all(f32[2,1,128,2048]{3,0,1,2:T(2,128)S(1)} %copy.202), channel_id=1, replica_groups=mesh['lat'=16,'lon'=8] {'lon'}, dimensions={2} | all-to-all | bytes 4194304 | tf_op jit(solution)/shard_map/all_to_all | solution.py:116
  714.3 14.4 %copy.265 = f32[2,16,128,128]{1,0,3,2:T(2,128)} copy(f32[2,16,128,128]{2,3,1,0:T(8,128)} %multiply_add_fusion.3) | data formatting | bytes 4194304 | tf_op jit(solution)/shard_map/reshape | solution.py:56
  728.7 24.8 %reshape.412 = f32[8,1,65536]{2,1,0:T(1,128)} reshape(f32[16384,1,2,16]{3,2,1,0:T(2,128)} %bitcast.335) | data formatting | bytes 4194304
  753.4 29.0 %all_to_all.271 = f32[8,1,65536]{2,1,0:T(1,128)} all-to-all(f32[8,1,65536]{2,1,0:T(1,128)} %reshape.412), channel_id=1, replica_groups=mesh['lat'=16,'lon'=8] {'lon'}, dimensions={0} | all-to-all | bytes 4194304 | tf_op jit(solution)/shard_map/all_to_all | solution.py:121
  782.4 8.5 reduce.10
  790.9 31.8 %reshape.413 = f32[16384,1,2,16]{3,2,1,0:T(2,128)} reshape(f32[8,65536]{1,0:T(8,128)} %reduce.10) | data formatting | bytes 4194304
  822.8 21.6 %copy.267 = f32[2,1,16,8,2048]{4,2,3,0,1:T(8,128)} copy(f32[2,1,16,8,2048]{2,0,4,3,1:T(2,128)} %bitcast.336) | data formatting | bytes 4194304 | tf_op jit(solution)/shard_map/all_to_all | solution.py:121
  844.4 6.1 bitcast_subtract_fusion.1
  854.6 36.3 %all_to_all.272 = f32[2,1,128,2048]{2,0,1,3:T(2,128)} all-to-all(f32[2,1,128,2048]{2,0,1,3:T(2,128)} %copy.216), channel_id=1, replica_groups=mesh['lat'=16,'lon'=8] {'lat'}, dimensions={3} | all-to-all | bytes 4194304 | tf_op jit(solution)/shard_map/all_to_all | solution.py:126
  899.6 7.6 copy.221
  907.2 31.8 %all_to_all.273 = f32[2,1,2048,128]{3,0,1,2:T(2,128)S(1)} all-to-all(f32[2,1,2048,128]{3,0,1,2:T(2,128)S(1)} %copy.221), channel_id=1, replica_groups=mesh['lat'=16,'lon'=8] {'lat'}, dimensions={2} | all-to-all | bytes 4194304 | tf_op jit(solution)/shard_map/all_to_all | solution.py:131
  968.6 10.6 fusion.29
  980.8 28.4 %all_to_all.274 = f32[2,1,128,2048]{3,0,1,2:T(2,128)S(1)} all-to-all(f32[2,1,128,2048]{3,0,1,2:T(2,128)S(1)} %copy.223), channel_id=1, replica_groups=mesh['lat'=16,'lon'=8] {'lon'}, dimensions={2} | all-to-all | bytes 4194304 | tf_op jit(solution)/shard_map/all_to_all | solution.py:116
  1025.7 14.4 %copy.270 = f32[2,16,128,128]{1,0,3,2:T(2,128)} copy(f32[2,16,128,128]{2,3,1,0:T(8,128)} %multiply_add_fusion.1) | data formatting | bytes 4194304 | tf_op jit(solution)/shard_map/reshape | solution.py:56
  1040.1 24.7 %reshape.414 = f32[8,1,65536]{2,1,0:T(1,128)} reshape(f32[16384,1,2,16]{3,2,1,0:T(2,128)} %bitcast.337) | data formatting | bytes 4194304
  1064.8 29.0 %all_to_all.275 = f32[8,1,65536]{2,1,0:T(1,128)} all-to-all(f32[8,1,65536]{2,1,0:T(1,128)} %reshape.414), channel_id=1, replica_groups=mesh['lat'=16,'lon'=8] {'lon'}, dimensions={0} | all-to-all | bytes 4194304 | tf_op jit(solution)/shard_map/all_to_all | solution.py:121
  1093.8 8.5 reduce.11
  1102.2 31.9 %reshape.415 = f32[16384,1,2,16]{3,2,1,0:T(2,128)} reshape(f32[8,65536]{1,0:T(8,128)} %reduce.11) | data formatting | bytes 4194304
  1134.1 21.6 %copy.272 = f32[2,1,16,8,2048]{4,2,3,0,1:T(8,128)} copy(f32[2,1,16,8,2048]{2,0,4,3,1:T(2,128)} %bitcast.338) | data formatting | bytes 4194304 | tf_op jit(solution)/shard_map/all_to_all | solution.py:121
  1155.7 6.1 bitcast_subtract_fusion
  1165.9 36.4 %all_to_all.276 = f32[2,1,128,2048]{2,0,1,3:T(2,128)} all-to-all(f32[2,1,128,2048]{2,0,1,3:T(2,128)} %copy.237), channel_id=1, replica_groups=mesh['lat'=16,'lon'=8] {'lat'}, dimensions={3} | all-to-all | bytes 4194304 | tf_op jit(solution)/shard_map/all_to_all | solution.py:126
  1210.9 7.6 copy.242
  1218.5 31.8 %all_to_all.277 = f32[2,1,2048,128]{3,0,1,2:T(2,128)S(1)} all-to-all(f32[2,1,2048,128]{3,0,1,2:T(2,128)S(1)} %copy.242), channel_id=1, replica_groups=mesh['lat'=16,'lon'=8] {'lat'}, dimensions={2} | all-to-all | bytes 4194304 | tf_op jit(solution)/shard_map/all_to_all | solution.py:131
  (214 shorter events, 253.5 us)
Async XLA Ops:
  0.0 84.5 %copy-start = (f32[2,256,256]{2,1,0:T(8,128)S(1)}, f32[2,256,256]{2,1,0:T(8,128)}, u32[]{:S(2)}) copy-start(f32[2,256,256]{2,1,0:T(8,128)} %param.12) | copy-start | bytes 1572868
  1.1 7.8 collective-permute-start.1
  6.8 5.9 collective-permute-start
  7.6 15.5 %copy-start.12 = (f32[2,2]{1,0:T(2,128)S(1)}, f32[2,2]{1,0:T(2,128)}, u32[]{:S(2)}) copy-start(f32[2,2]{1,0:T(2,128)} %param.10) | copy-start | bytes 52
  15.7 7.4 copy-start.5
  15.7 8.7 copy-start.1
  15.8 8.7 collective-permute-start.2
  20.0 4.4 collective-permute-start.3
  39.8 5.0 copy-start.10
  39.8 31.3 %all-to-all-start = ((f32[2,1,128,2048]{3,0,1,2:T(2,128)}), f32[2,1,128,2048]{3,0,1,2:T(2,128)}, u32[]{:S(2)}, u32[]{:S(2)}) async-start(f32[2,1,128,2048]{3,0,1,2:T(2,128)} %copy.159), calls=%async_computation | async-start | bytes 4194304 | tf_op jit(solution)/shard_map/all_to_all | solution.py:116
  82.9 1.4 copy-start.6
  229.0 37.9 %all-to-all-start.2 = ((f32[2,1,128,2048]{2,0,1,3:T(2,128)}), f32[2,1,128,2048]{2,0,1,3:T(2,128)}, u32[]{:S(2)}, u32[]{:S(2)}) async-start(f32[2,1,128,2048]{2,0,1,3:T(2,128)} %copy.173), calls=%async_computation.2 | async-start | bytes 4194304 | tf_op jit(solution)/shard_map/all_to_all | solution.py:126
  271.0 3.7 copy-start.11
  324.4 1.3 copy-start.3
  325.8 3.9 collective-permute-start.5
  326.2 5.9 collective-permute-start.4
  337.1 6.4 collective-permute-start.6
  341.5 3.1 collective-permute-start.7
  394.4 1.3 copy-start.8
  631.5 1.3 copy-start.2
  633.0 4.1 collective-permute-start.9
  635.1 5.9 collective-permute-start.8
  646.1 6.3 collective-permute-start.10
  650.5 3.1 collective-permute-start.11
  707.8 1.4 copy-start.9
  946.9 1.3 copy-start.4
  948.4 3.9 collective-permute-start.13
  950.2 5.9 collective-permute-start.12
  961.2 6.3 collective-permute-start.14
  965.6 3.1 collective-permute-start.15
  1019.3 1.3 copy-start.7
where the time goes:
time: 1270 us; the launch traced here: 1260 us
  local copies, waits for them, and re-layouts  524 us (41%)
  blocking collectives  441 us (35%)
  other arithmetic  130 us (10%)
  waiting for transfers between devices  79.7 us (6%)
  starting transfers between devices  51.7 us (4%)
  matrix products  31.6 us (2%)
    unnamed x34, local copies, waits for them, and re-layouts  236 us
    all_to_all x4, blocking collectives, lat_lines_solve(): lax.all_to_all(finished, 'lat', split_axis=2, concat_axis=3, tiled=True)  129 us
    all_to_all x4, blocking collectives, lon_lines_solve(): lax.all_to_all(finished, 'lon', split_axis=3, concat_axis=2, tiled=True)  117 us
    all_to_all x3, blocking collectives, lat_lines_solve(): lax.all_to_all(values, 'lat', split_axis=3, concat_axis=2, tiled=True)  110 us
    all_to_all x5, local copies, waits for them, and re-layouts, lon_lines_solve(): lax.all_to_all(finished, 'lon', split_axis=3, concat_axis=2, tiled=True)  86.9 us
    all_to_all x3, blocking collectives, lon_lines_solve(): lax.all_to_all(values, 'lon', split_axis=2, concat_axis=3, tiled=True)  84.8 us
    reshape x4, local copies, waits for them, and re-layouts, lon_finish(): return result.reshape(result.shape[:3] + (-1,))  57.4 us
    all_to_all x4, other arithmetic, lon_lines_solve(): lax.all_to_all(finished, 'lon', split_axis=3, concat_axis=2, tiled=True)  33.9 us
  transfers between devices with their start and end apart: 18, of which 13 were waited for; matrix products, arithmetic and copies ran while one was open for 0% of the time, Pallas kernels for 0%

commit v1 on v0

--- a/solution.py
+++ b/solution.py
@@ -118,7 +118,10 @@
         reduced,
         rate_lon,
     )
-    return lax.all_to_all(finished, "lon", split_axis=3, concat_axis=2, tiled=True)
+    return jnp.concatenate(
+        lax.all_to_all(jnp.stack(jnp.split(finished, lax.axis_size("lon"), axis=3)), "lon", 0, 0),
+        axis=2,
+    )
 
 
 def lat_lines_solve(values, inverse, reduced, rate_lat):

time: 1270 us -> 907 us (0.71)
  local copies, waits for them, and re-layouts: 524 us -> 215 us
  other arithmetic: 130 us -> 82.3 us
    unnamed x34 -> x66, local copies, waits for them, and re-layouts: 236 us -> 42.1 us
    all_to_all x5 -> x0, local copies, waits for them, and re-layouts: 86.9 us -> none  [lon_lines_solve(): lax.all_to_all(finished, 'lon', split_axis=3, concat_axis=2, tiled=True)]
    reshape x4, local copies, waits for them, and re-layouts: 57.4 us -> 11 us  [lon_finish(): return result.reshape(result.shape[:3] + (-1,))]
    all_to_all x4 -> x0, other arithmetic: 33.9 us -> none  [lon_lines_solve(): lax.all_to_all(finished, 'lon', split_axis=3, concat_axis=2, tiled=True)]
  transfers between devices with their start and end apart: 18 -> 18, of which waited for: 13 -> 14; matrix products, arithmetic and copies ran while one was open for 0% -> 0% of each run, Pallas kernels for 0% -> 0%
where the time goes in v1:
time: 907 us; the launch traced here: 898 us
  blocking collectives  437 us (48%)
  local copies, waits for them, and re-layouts  215 us (24%)
  other arithmetic  82.3 us (9%)
  waiting for transfers between devices  79.3 us (9%)
  starting transfers between devices  51.2 us (6%)
  matrix products  31.6 us (3%)
    all_to_all x4, blocking collectives, lat_lines_solve(): lax.all_to_all(finished, 'lat', split_axis=2, concat_axis=3, tiled=True)  129 us
    all_to_all x4, blocking collectives, lon_lines_solve(): lax.all_to_all(jnp.stack(jnp.split(finished, lax.axis_size('lon'), axis=3...  118 us
    all_to_all x3, blocking collectives, lat_lines_solve(): lax.all_to_all(values, 'lat', split_axis=3, concat_axis=2, tiled=True)  105 us
    all_to_all x3, blocking collectives, lon_lines_solve(): lax.all_to_all(values, 'lon', split_axis=2, concat_axis=3, tiled=True)  84.8 us
    unnamed x66, local copies, waits for them, and re-layouts  42.1 us
    reshape x4, local copies, waits for them, and re-layouts, lat_finish(): return result.reshape((dims[0], dims[1], dims[2] * dims[3], dims[4]))  30.4 us
    all_to_all x1, waiting for transfers between devices, lat_lines_solve(): lax.all_to_all(values, 'lat', split_axis=3, concat_axis=2, tiled=True)  28.4 us
    sub x2, other arithmetic, shards(): first_lon = solve_lon(start_value - scale_lon * along_lon)  26.2 us
  transfers between devices with their start and end apart: 18, of which 14 were waited for; matrix products, arithmetic and copies ran while one was open for 0% of the time, Pallas kernels for 0%

profile of v1, /device:TPU:1, one launch (start us, length us, event | category | flops | bytes accessed | tf_op | source)
XLA Modules:
  0.0 898.4 jit_solution(9806654872759436931)
XLA Ops:
  1.1 5.7 collective-permute-start.1
  9.0 3.8 collective-permute-done
  12.7 4.0 concatenate.114
  17.9 4.0 collective-permute-start.2
  25.8 12.5 %multiply_subtract_fusion.1 = (f32[2,1,128,2048]{3,2,0,1:T(8,128)S(1)}, f32[2,1,128,2048]{3,2,0,1:T(8,128)}, f32[2,1,128,2048]{3,2,0,1:T(8,128)}) fusion(f32[2]{0:T(128)S(1)} %get-tuple-element.65, f32[2,1,128,2048]{3,2,0,1:T(8,128)S(1)} %bitcast.446, f32[2,1,128,1]{3,2,0,1:T(8,128)S(1)} %collective-permute-done, ...), kind=kLoop, calls=%fused_computation.110 | loop fusion | flops 13631488 | bytes 15765560 | tf_op jit(solution)/shard_map/sub | solution.py:162
  41.2 4.7 all-to-all-start
  46.1 26.0 %all-to-all-done = f32[2,1,128,2048]{3,0,1,2:T(2,128)} async-done(((f32[2,1,128,2048]{3,0,1,2:T(2,128)}), f32[2,1,128,2048]{3,0,1,2:T(2,128)}, u32[]{:S(2)}, u32[]{:S(2)}) %all-to-all-start) | async-done | bytes 2097184 | tf_op jit(solution)/shard_map/all_to_all | solution.py:116
  103.8 28.9 %all_to_all.212 = f32[8,2,1,16,2048]{4,3,1,2,0:T(8,128)S(1)} all-to-all(f32[8,2,1,16,2048]{4,3,1,2,0:T(8,128)S(1)} %fusion.92), channel_id=1, replica_groups=mesh['lat'=16,'lon'=8] {'lon'}, dimensions={0} | all-to-all | bytes 4194304 | tf_op jit(solution)/shard_map/all_to_all | solution.py:122
  136.0 4.2 copy.199
  140.1 9.3 %all-to-all-start.2 = ((f32[2,1,128,2048]{2,0,1,3:T(2,128)}), f32[2,1,128,2048]{2,0,1,3:T(2,128)}, u32[]{:S(2)}, u32[]{:S(2)}) async-start(f32[2,1,128,2048]{2,0,1,3:T(2,128)} %copy.199), calls=%async_computation.2 | async-start | bytes 4194304 | tf_op jit(solution)/shard_map/all_to_all | solution.py:129
  149.6 28.4 %all-to-all-done.2 = f32[2,1,128,2048]{2,0,1,3:T(2,128)} async-done(((f32[2,1,128,2048]{2,0,1,3:T(2,128)}), f32[2,1,128,2048]{2,0,1,3:T(2,128)}, u32[]{:S(2)}, u32[]{:S(2)}) %all-to-all-start.2) | async-done | bytes 2097184 | tf_op jit(solution)/shard_map/all_to_all | solution.py:129
  178.0 4.2 copy.201
  182.2 3.6 fusion.56
  186.7 7.6 copy.204
  194.3 33.5 %all_to_all.213 = f32[2,1,2048,128]{3,0,1,2:T(2,128)S(1)} all-to-all(f32[2,1,2048,128]{3,0,1,2:T(2,128)S(1)} %copy.204), channel_id=1, replica_groups=mesh['lat'=16,'lon'=8] {'lat'}, dimensions={2} | all-to-all | bytes 4194304 | tf_op jit(solution)/shard_map/all_to_all | solution.py:134
  243.4 4.0 concatenate.123
  248.4 4.4 collective-permute-start.6
  255.9 9.8 %fusion.37 = f32[2,1,128,2048]{3,2,0,1:T(8,128)S(1)} fusion(f32[2,1,128,2048]{3,2,0,1:T(8,128)} %get-tuple-element.12, f32[2,1,1,2050]{3,2,0,1:T(1,128)S(1)} %collective-permute-done.7, f32[2,1,128,2050]{3,2,0,1:T(8,128)} %concatenate.123, f32[2,1,1,2050]{3,2,0,1:T(1,128)S(1)} %collective-permute-done.6, f32[2,128,2048]{2,1,0:T(8,128)} %param.8, ...), kind=kLoop, calls=%fused_computation.61 | loop fusion | flops 8912896 | bytes 10522664 | tf_op jit(solution)/shard_map/sub | solution.py:166
  267.4 28.1 %all_to_all.214 = f32[2,1,128,2048]{3,0,1,2:T(2,128)S(1)} all-to-all(f32[2,1,128,2048]{3,0,1,2:T(2,128)S(1)} %copy.207), channel_id=1, replica_groups=mesh['lat'=16,'lon'=8] {'lon'}, dimensions={2} | all-to-all | bytes 4194304 | tf_op jit(solution)/shard_map/all_to_all | solution.py:116
  301.9 3.6 fusion.108
  325.4 29.7 %all_to_all.215 = f32[8,2,1,16,2048]{4,3,1,2,0:T(8,128)S(1)} all-to-all(f32[8,2,1,16,2048]{4,3,1,2,0:T(8,128)S(1)} %fusion.84), channel_id=1, replica_groups=mesh['lat'=16,'lon'=8] {'lon'}, dimensions={0} | all-to-all | bytes 4194304 | tf_op jit(solution)/shard_map/all_to_all | solution.py:122
  358.3 4.1 copy.219
  362.5 35.1 %all_to_all.216 = f32[2,1,128,2048]{2,0,1,3:T(2,128)} all-to-all(f32[2,1,128,2048]{2,0,1,3:T(2,128)} %copy.219), channel_id=1, replica_groups=mesh['lat'=16,'lon'=8] {'lat'}, dimensions={3} | all-to-all | bytes 4194304 | tf_op jit(solution)/shard_map/all_to_all | solution.py:129
  397.6 4.1 copy.221
  406.2 7.6 copy.224
  413.8 31.9 %all_to_all.217 = f32[2,1,2048,128]{3,0,1,2:T(2,128)S(1)} all-to-all(f32[2,1,2048,128]{3,0,1,2:T(2,128)S(1)} %copy.224), channel_id=1, replica_groups=mesh['lat'=16,'lon'=8] {'lat'}, dimensions={2} | all-to-all | bytes 4194304 | tf_op jit(solution)/shard_map/all_to_all | solution.py:134
  458.1 3.8 collective-permute-done.8
  461.9 4.0 concatenate.130
  466.9 4.4 collective-permute-start.10
  474.4 13.8 %multiply_subtract_fusion = (f32[2,1,128,2048]{3,2,0,1:T(8,128)S(1)}, f32[2,1,128,2048]{3,2,0,1:T(8,128)}) fusion(f32[2]{0:T(128)S(1)} %get-tuple-element.65, f32[2,1,128,2048]{3,2,0,1:T(8,128)} %copy-done.6, f32[2,1,128,1]{3,2,0,1:T(8,128)S(1)} %collective-permute-done.8, f32[2,1,128,1]{3,2,0,1:T(8,128)S(1)} %collective-permute-done.9, ...), kind=kLoop, calls=%fused_computation.109 | loop fusion | flops 13107200 | bytes 11571256 | tf_op jit(solution)/shard_map/sub | solution.py:162
  489.8 28.4 %all_to_all.218 = f32[2,1,128,2048]{3,0,1,2:T(2,128)S(1)} all-to-all(f32[2,1,128,2048]{3,0,1,2:T(2,128)S(1)} %copy.226), channel_id=1, replica_groups=mesh['lat'=16,'lon'=8] {'lon'}, dimensions={2} | all-to-all | bytes 4194304 | tf_op jit(solution)/shard_map/all_to_all | solution.py:116
  524.6 3.6 fusion.106
  548.1 30.0 %all_to_all.219 = f32[8,2,1,16,2048]{4,3,1,2,0:T(8,128)S(1)} all-to-all(f32[8,2,1,16,2048]{4,3,1,2,0:T(8,128)S(1)} %fusion.76), channel_id=1, replica_groups=mesh['lat'=16,'lon'=8] {'lon'}, dimensions={0} | all-to-all | bytes 4194304 | tf_op jit(solution)/shard_map/all_to_all | solution.py:122
  582.4 4.1 copy.238
  586.5 35.0 %all_to_all.220 = f32[2,1,128,2048]{2,0,1,3:T(2,128)} all-to-all(f32[2,1,128,2048]{2,0,1,3:T(2,128)} %copy.238), channel_id=1, replica_groups=mesh['lat'=16,'lon'=8] {'lat'}, dimensions={3} | all-to-all | bytes 4194304 | tf_op jit(solution)/shard_map/all_to_all | solution.py:129
  621.6 4.1 copy.240
  630.2 7.6 copy.243
  637.8 31.9 %all_to_all.221 = f32[2,1,2048,128]{3,0,1,2:T(2,128)S(1)} all-to-all(f32[2,1,2048,128]{3,0,1,2:T(2,128)S(1)} %copy.243), channel_id=1, replica_groups=mesh['lat'=16,'lon'=8] {'lat'}, dimensions={2} | all-to-all | bytes 4194304 | tf_op jit(solution)/shard_map/all_to_all | solution.py:134
  686.2 4.0 concatenate.139
  691.2 4.4 collective-permute-start.14
  698.7 9.7 %fusion.29 = f32[2,1,128,2048]{3,2,0,1:T(8,128)S(1)} fusion(f32[2,1,128,2048]{3,2,0,1:T(8,128)} %get-tuple-element.10, f32[2,1,1,2050]{3,2,0,1:T(1,128)S(1)} %collective-permute-done.15, f32[2,1,128,2050]{3,2,0,1:T(8,128)} %concatenate.139, f32[2,1,1,2050]{3,2,0,1:T(1,128)S(1)} %collective-permute-done.14, f32[2,128,2048]{2,1,0:T(8,128)} %param.8, ...), kind=kLoop, calls=%fused_computation.53 | loop fusion | flops 8912896 | bytes 10522664 | tf_op jit(solution)/shard_map/sub | solution.py:166
  710.0 28.4 %all_to_all.222 = f32[2,1,128,2048]{3,0,1,2:T(2,128)S(1)} all-to-all(f32[2,1,128,2048]{3,0,1,2:T(2,128)S(1)} %copy.245), channel_id=1, replica_groups=mesh['lat'=16,'lon'=8] {'lon'}, dimensions={2} | all-to-all | bytes 4194304 | tf_op jit(solution)/shard_map/all_to_all | solution.py:116
  768.3 29.8 %all_to_all.223 = f32[8,2,1,16,2048]{4,3,1,2,0:T(8,128)S(1)} all-to-all(f32[8,2,1,16,2048]{4,3,1,2,0:T(8,128)S(1)} %fusion.68), channel_id=1, replica_groups=mesh['lat'=16,'lon'=8] {'lon'}, dimensions={0} | all-to-all | bytes 4194304 | tf_op jit(solution)/shard_map/all_to_all | solution.py:122
  802.5 4.1 copy.257
  806.6 35.0 %all_to_all.224 = f32[2,1,128,2048]{2,0,1,3:T(2,128)} all-to-all(f32[2,1,128,2048]{2,0,1,3:T(2,128)} %copy.257), channel_id=1, replica_groups=mesh['lat'=16,'lon'=8] {'lat'}, dimensions={3} | all-to-all | bytes 4194304 | tf_op jit(solution)/shard_map/all_to_all | solution.py:129
  841.6 4.1 copy.259
  850.2 7.6 copy.262
  857.8 31.9 %all_to_all.225 = f32[2,1,2048,128]{3,0,1,2:T(2,128)S(1)} all-to-all(f32[2,1,2048,128]{3,0,1,2:T(2,128)S(1)} %copy.262), channel_id=1, replica_groups=mesh['lat'=16,'lon'=8] {'lat'}, dimensions={2} | all-to-all | bytes 4194304 | tf_op jit(solution)/shard_map/all_to_all | solution.py:134
  (249 shorter events, 224.8 us)
Async XLA Ops:
  0.0 85.4 %copy-start = (f32[2,256,256]{2,1,0:T(8,128)S(1)}, f32[2,256,256]{2,1,0:T(8,128)}, u32[]{:S(2)}) copy-start(f32[2,256,256]{2,1,0:T(8,128)} %param.12) | copy-start | bytes 1572868
  1.1 7.8 collective-permute-start.1
  6.8 5.9 collective-permute-start
  7.6 17.4 %copy-start.18 = (f32[2,2]{1,0:T(2,128)S(1)}, f32[2,2]{1,0:T(2,128)}, u32[]{:S(2)}) copy-start(f32[2,2]{1,0:T(2,128)} %param.10) | copy-start | bytes 52
  7.6 17.4 %copy-start.16 = (s32[128,2048]{1,0:T(8,128)S(1)}, s32[128,2048]{1,0:T(8,128)}, u32[]{:S(2)}) copy-start(s32[128,2048]{1,0:T(8,128)} %param.9) | copy-start | bytes 3145732
  16.7 9.1 %copy-start.1 = (f32[2,1,128,2048]{3,2,1,0:T(8,128)S(1)}, f32[2,1,128,2048]{3,2,1,0:T(8,128)}, u32[]{:S(2)}) copy-start(f32[2,1,128,2048]{3,2,1,0:T(8,128)} %param.7) | copy-start | bytes 6291460
  17.9 7.2 collective-permute-start.2
  21.9 3.9 collective-permute-start.3
  41.2 4.7 copy-start.15
  41.2 30.9 %all-to-all-start = ((f32[2,1,128,2048]{3,0,1,2:T(2,128)}), f32[2,1,128,2048]{3,0,1,2:T(2,128)}, u32[]{:S(2)}, u32[]{:S(2)}) async-start(f32[2,1,128,2048]{3,0,1,2:T(2,128)} %copy.187), calls=%async_computation | async-start | bytes 4194304 | tf_op jit(solution)/shard_map/all_to_all | solution.py:116
  83.8 1.4 copy-start.11
  132.7 1.6 copy-start.7
  140.1 37.9 %all-to-all-start.2 = ((f32[2,1,128,2048]{2,0,1,3:T(2,128)}), f32[2,1,128,2048]{2,0,1,3:T(2,128)}, u32[]{:S(2)}, u32[]{:S(2)}) async-start(f32[2,1,128,2048]{2,0,1,3:T(2,128)} %copy.199), calls=%async_computation.2 | async-start | bytes 4194304 | tf_op jit(solution)/shard_map/all_to_all | solution.py:129
  182.2 3.7 copy-start.17
  235.6 1.4 copy-start.9
  237.1 3.9 collective-permute-start.5
  237.5 5.9 collective-permute-start.4
  248.4 6.8 collective-permute-start.6
  252.8 3.1 collective-permute-start.7
  305.5 1.3 copy-start.13
  355.1 1.6 copy-start.8
  452.8 1.3 copy-start.6
  454.2 3.9 collective-permute-start.9
  456.0 5.9 collective-permute-start.8
  466.9 6.5 collective-permute-start.10
  471.3 3.1 collective-permute-start.11
  528.2 1.3 copy-start.14
  548.1 30.2 %copy-start.4 = (f32[2,1,128,2050]{3,2,0,1:T(8,128)S(1)}, f32[2,1,128,2050]{3,2,0,1:T(8,128)}, u32[]{:S(2)}) copy-start(f32[2,1,128,2050]{3,2,0,1:T(8,128)} %concatenate.130) | copy-start | bytes 6297604
  578.1 1.6 copy-start.2
  677.6 1.3 copy-start.10
  679.0 3.9 collective-permute-start.13
  680.1 6.1 collective-permute-start.12
  691.2 6.3 collective-permute-start.14
  695.6 3.1 collective-permute-start.15
  748.5 1.3 copy-start.12
  768.3 30.0 %copy-start.5 = (f32[2,1,128,2050]{3,2,0,1:T(8,128)S(1)}, f32[2,1,128,2050]{3,2,0,1:T(8,128)}, u32[]{:S(2)}) copy-start(f32[2,1,128,2050]{3,2,0,1:T(8,128)} %concatenate.130) | copy-start | bytes 6297604
  798.1 1.6 copy-start.3
